TPU v7x, 256 devices: a whole 4x4x8 slice. The times are simulated.
256 devices in a mesh: dp: 64 (over x, z, core), mp: 4 (over y).
Axes of the slice: x: 4, y: 4, z: 8, core: 2. Of those that a mesh axis runs over, the one named last changes fastest.
Arguments:
- gradient: bfloat16 [128, 1024, 1024], P('dp', 'mp'), may hold values from -3 to 3
- left_codes: bfloat16 [128, 1024, 1024], P('dp', 'mp'), may hold values from -1 to 1
- left_scales: bfloat16 [128, 1024], P('dp', 'mp'), may hold values from 0.5 to 5
- right_codes: bfloat16 [128, 1024, 1024], P('dp', 'mp'), may hold values from -1 to 1
- right_scales: bfloat16 [128, 1024], P('dp', 'mp'), may hold values from 0.5 to 5
- left_root_codes: bfloat16 [128, 1024, 1024], P('dp', 'mp'), may hold values from -0.1 to 1, as said below
- left_root_scales: bfloat16 [128, 1024], P('dp', 'mp'), may hold values from 0.5 to 2
- right_root_codes: bfloat16 [128, 1024, 1024], P('dp', 'mp'), may hold values from -0.1 to 1, as said below
- right_root_scales: bfloat16 [128, 1024], P('dp', 'mp'), may hold values from 0.5 to 2
- owner_plan: int32 [128], replicated, may hold values from 0 to 127, as said below
Outputs:
- new_left_codes: bfloat16 [128, 1024, 1024], P('dp', 'mp')
- new_left_scales: bfloat16 [128, 1024], P('dp', 'mp')
- new_right_codes: bfloat16 [128, 1024, 1024], P('dp', 'mp')
- new_right_scales: bfloat16 [128, 1024], P('dp', 'mp')
- update: bfloat16 [128, 1024, 1024], P('dp', 'mp')
Inputs may be any that keep to these rules, and one draw needn't show every extreme that they name: `left_root_codes`: each row i has one entry on the diagonal between 0.6 and 1 and small entries elsewhere. `right_root_codes`: each row i has one entry on the diagonal between 0.6 and 1 and small entries elsewhere. `owner_plan`: A permutation of the 128 slots; slot s lies on device s // 2 of dp. Exactly 12 blocks get a slot on another device; from each device at most one block leaves and at most one arrives, and an arriving block takes the slot that the device's leaving block frees; every other block keeps its slot.
All inputs are finite; a program needn't handle non-finite values. Where the computation divides by a largest or mean magnitude, that divisor is 1e-20 or more.
Results may differ from a plain program's by a relative error of at most 0.009.
Values may be sent and summed in bfloat16 or wider, within the bound.
A program may use at most 64 MiB of HBM per device.

v0:
```python
import math
import jax
import jax.numpy as jnp
from jax import lax
from jax.sharding import PartitionSpec as P

DECAY = 0.95
EPSILON = 1e-06


def side_by_side(arrays, axis, dim, along):
    widths = [math.prod(a.shape[along:]) for a in arrays]
    both = jnp.concatenate(
        [a.reshape(*a.shape[:along], w) for a, w in zip(arrays, widths)], axis=along
    )
    result = lax.all_gather(both, axis, axis=dim, tiled=True)
    tiles = jnp.split(result, [sum(widths[:k]) for k in range(1, len(widths))], axis=along)
    return tuple(
        (b.reshape(*result.shape[:along], *a.shape[along:]) for a, b in zip(arrays, tiles))
    )


def in_one_piece(arrays, axis, split_dim, concat_dim, along):
    columns = [a.reshape(*a.shape[:along], -1) for a in arrays]
    both = jnp.concatenate(columns, axis=along)
    result, at, done = (
        lax.all_to_all(both, axis, split_axis=split_dim, concat_axis=concat_dim, tiled=True),
        0,
        [],
    )
    for a, column in zip(arrays, columns):
        slab = result[..., at : at + column.shape[along]]
        done.append(slab.reshape(*slab.shape[:along], *a.shape[along:]))
        at += column.shape[along]
    return tuple(done)


def dequantize(codes, scales):
    return codes.astype(jnp.float32) * scales.astype(jnp.float32)[..., None]


def requantize(matrix):
    scales = (jnp.max(jnp.abs(matrix), axis=-1) + EPSILON).astype(jnp.bfloat16)
    codes = (matrix / scales.astype(jnp.float32)[..., None]).astype(jnp.bfloat16)
    return (codes, scales)


def refresh(
    gradient,
    left_codes,
    left_scales,
    right_codes,
    right_scales,
    left_root_codes,
    left_root_scales,
    right_root_codes,
    right_root_scales,
):
    gathered = lax.all_gather(gradient, "mp", axis=1, tiled=True)
    height = gradient.shape[1]
    offset = lax.axis_index("mp") * height
    left_new = DECAY * dequantize(left_codes, left_scales) + jnp.einsum(
        "sik,sjk->sij", gradient, gathered, preferred_element_type=jnp.float32
    )
    columns = lax.dynamic_slice_in_dim(gathered, offset, height, 2)
    right_new = DECAY * dequantize(right_codes, right_scales) + jnp.einsum(
        "sji,sjk->sik", columns, gathered, preferred_element_type=jnp.float32
    )
    left_root = dequantize(left_root_codes, left_root_scales).astype(jnp.bfloat16)
    lifted = jnp.einsum(
        "sik,skj->sij", left_root, gathered, preferred_element_type=jnp.float32
    ).astype(jnp.bfloat16)
    code_piece, scale_piece = side_by_side((right_root_codes, right_root_scales), "mp", 1, 2)
    root_piece = dequantize(code_piece, scale_piece).astype(jnp.bfloat16)
    direction = jnp.einsum("sik,skj->sij", lifted, root_piece, preferred_element_type=jnp.float32)
    grad_square = jnp.sum(jnp.square(gradient.astype(jnp.float32)), axis=(1, 2))
    dir_square = jnp.sum(jnp.square(direction), axis=(1, 2))
    grad_total, dir_total = lax.psum((grad_square, dir_square), "mp")
    scaling = jnp.sqrt(grad_total + EPSILON) / jnp.sqrt(dir_total + EPSILON)
    update = (direction * scaling[:, None, None]).astype(jnp.bfloat16)
    left_out, left_scale = requantize(left_new)
    right_out, right_scale = requantize(right_new)
    return (update, left_out, left_scale, right_out, right_scale)


def routing(owner_plan, slot_count):
    owners = lax.axis_size("dp")
    myself = lax.axis_index("dp")
    blocks = jnp.arange(owner_plan.shape[0], dtype=jnp.int32)
    anchors = blocks // slot_count
    targets = owner_plan // slot_count
    moving = anchors != targets
    leaving = moving & (anchors == myself)
    vacancy = jnp.sum(jnp.where(leaving, blocks % slot_count, 0))
    present = jnp.any(leaving)
    device_ids = jnp.arange(owners, dtype=jnp.int32)
    forward = jnp.sum(
        jnp.where(moving[:, None] & (targets[:, None] == device_ids[None, :]), anchors[:, None], 0),
        axis=0,
    )
    backward = jnp.sum(
        jnp.where(moving[:, None] & (anchors[:, None] == device_ids[None, :]), targets[:, None], 0),
        axis=0,
    )
    retain = present & (jnp.arange(slot_count, dtype=jnp.int32) == vacancy)
    return (forward[:, None], backward[:, None], vacancy, retain)


def outgoing(values, vacancy):
    return lax.dynamic_slice_in_dim(values, vacancy, 1, 0)


def landing(values, arrived, retain):
    layout = [1] * values.ndim
    layout[0] = values.shape[0]
    return jnp.where(retain.reshape(layout), arrived, values)


def spread_states(stacked, stacked_scales, chooser):
    data_parts, scale_parts = in_one_piece((stacked, stacked_scales), "dp", 2, 1, 3)
    data_back, scale_back = in_one_piece(
        (data_parts[:, chooser], scale_parts[:, chooser]), "dp", 1, 3, 4
    )
    return (data_back[:, 0], scale_back[:, 0])


def local(
    gradient,
    left_codes,
    left_scales,
    right_codes,
    right_scales,
    left_root_codes,
    left_root_scales,
    right_root_codes,
    right_root_scales,
    owner_plan,
):
    slot_count = gradient.shape[0]
    forward, backward, vacancy, retain = routing(owner_plan, slot_count)
    update, left_out, left_scale, right_out, right_scale = refresh(
        gradient,
        left_codes,
        left_scales,
        right_codes,
        right_scales,
        left_root_codes,
        left_root_scales,
        right_root_codes,
        right_root_scales,
    )
    stacked = jnp.stack([outgoing(left_out, vacancy), outgoing(right_out, vacancy)])
    stacked_scales = jnp.stack([outgoing(left_scale, vacancy), outgoing(right_scale, vacancy)])
    data_back, scale_back = spread_states(stacked, stacked_scales, forward)
    new_left = landing(left_out, data_back[0], retain)
    new_left_scale = landing(left_scale, scale_back[0], retain)
    new_right = landing(right_out, data_back[1], retain)
    new_right_scale = landing(right_scale, scale_back[1], retain)
    return (new_left, new_left_scale, new_right, new_right_scale, update)


def solution(mesh):
    placed = (
        P("dp", "mp", None),
        P("dp", "mp", None),
        P("dp", "mp"),
        P("dp", "mp", None),
        P("dp", "mp"),
        P("dp", "mp", None),
        P("dp", "mp"),
        P("dp", "mp", None),
        P("dp", "mp"),
        P(),
    )
    return jax.shard_map(
        local,
        mesh=mesh,
        in_specs=placed,
        out_specs=(
            P("dp", "mp", None),
            P("dp", "mp"),
            P("dp", "mp", None),
            P("dp", "mp"),
            P("dp", "mp", None),
        ),
        check_vma=False,
    )
```

profile of v0, /device:TPU:1, one launch (start us, length us, event | category | flops | bytes accessed | tf_op | source)
XLA Modules:
  0.0 179.1 jit_solution(12612929652434687628)
XLA Ops:
  7.2 0.0 all-gather.3.cloned.1.call-start
  7.2 0.7 all-gather.3.cloned.1.call-update
  7.9 0.0 copy-start.8
  7.9 0.0 copy-start.3
  7.9 0.0 copy-start.4
  7.9 0.0 all-gather.5.cloned.1.call-start
  8.0 0.9 copy.68
  8.8 2.3 %pad_maximum_fusion.1 = bf16[2,256,1025]{2,1,0:T(8,128)(2,1)} fusion(bf16[2,256,1]{2,1,0:T(8,128)(2,1)S(1)} %copy.68, bf16[2,256,1024]{2,1,0:T(8,128)(2,1)} %param.17), kind=kLoop, calls=%fused_computation.19 | loop fusion | flops 2099200 | bytes 2099200 | tf_op jit(solution)/shard_map/concatenate | solution.py:13
  11.2 0.0 all-gather.5.cloned.1.call-update
  11.2 0.0 copy-done.8
  11.2 0.6 fusion.10
  13.2 0.0 copy-done.3
  13.2 0.0 copy-done.4
  13.9 0.0 copy-start.2
  13.9 50.6 %all-gather.3.cloned.1.call-done = bf16[2,1024,1024]{2,1,0:T(8,128)(2,1)} async-done(((bf16[2,256,1024]{2,1,0:T(8,128)(2,1)}), bf16[2,1024,1024]{2,1,0:T(8,128)(2,1)}) %all-gather.3.cloned.1.call-update) | async-done | bytes 4194320 | tf_op jit(solution)/shard_map/all_gather | solution.py:59
  64.5 0.0 copy-start.6
  64.5 0.0 copy-start.7
  64.5 4.5 %abs_reduce_fusion = (f32[2,256]{1,0:T(2,128)S(1)}, f32[2,256,1024]{2,1,0:T(8,128)S(1)}) fusion(bf16[2,1024,1024]{2,1,0:T(8,128)(2,1)} %all-gather.3.cloned.1.call-done, s32[]{:T(128)S(6)} %select_n.72, f32[2,256]{1,0:T(2,128)S(1)} %convert_element_type.78, bf16[2,256,1024]{2,1,0:T(8,128)(2,1)} %param.13), kind=kOutput, calls=%fused_computation.11 | convolution fusion | flops 1076887040 | bytes 8392708 | tf_op jit(solution)/shard_map/sji,sjk->sik/dot_general | solution.py:66
  69.0 0.0 copy-done.2
  69.0 0.0 copy-done.6
  69.0 0.0 copy-done.7
  69.0 1.5 abs_reduce_fusion.1
  70.5 0.0 copy-start
  70.6 0.1 reshape.123
  70.7 0.3 divide_convert_fusion.1
  71.0 0.3 divide_convert_fusion
  71.3 0.6 copy-done
  71.9 0.1 dynamic-slice_bitcast_fusion
  72.0 0.1 pad_maximum_fusion
  72.1 2.3 %copy.60 = bf16[2,1,256,1025]{3,0,1,2:T(2,128)(2,1)} copy(bf16[2,1,256,1025]{3,2,1,0:T(8,128)(2,1)S(1)} %pad_maximum_fusion) | data formatting | bytes 2099200 | tf_op jit(solution)/shard_map/concatenate | solution.py:25
  74.4 10.7 %all-to-all-start = ((bf16[2,1,256,1025]{3,0,1,2:T(2,128)(2,1)}), bf16[2,1,256,1025]{3,0,1,2:T(2,128)(2,1)S(1)}, u32[]{:S(2)}, u32[]{:S(2)}) async-start(bf16[2,1,256,1025]{3,0,1,2:T(2,128)(2,1)} %copy.60), calls=%async_computation | async-start | bytes 2359296 | tf_op jit(solution)/shard_map/all_to_all | solution.py:27
  85.1 0.1 select_reduce_fusion
  85.2 31.2 %all-to-all-done = bf16[2,1,256,1025]{3,0,1,2:T(2,128)(2,1)S(1)} async-done(((bf16[2,1,256,1025]{3,0,1,2:T(2,128)(2,1)}), bf16[2,1,256,1025]{3,0,1,2:T(2,128)(2,1)S(1)}, u32[]{:S(2)}, u32[]{:S(2)}) %all-to-all-start) | async-done | bytes 1049632 | tf_op jit(solution)/shard_map/all_to_all | solution.py:27
  116.4 0.1 slice.39
  116.5 2.1 %slice.38 = bf16[2,64,4,1024]{3,0,2,1:T(2,128)(2,1)} slice(bf16[2,64,4,1025]{3,0,2,1:T(2,128)(2,1)S(1)} %bitcast.37), slice={[0:2], [0:64], [0:4], [0:1024]} | slice | bytes 2097152 | tf_op jit(solution)/shard_map/slice | solution.py:32
  118.7 0.1 copy.62
  118.8 2.6 %copy.74 = bf16[2,64,4,1024]{3,2,1,0:T(4,128)(2,1)} copy(bf16[2,64,4,1024]{3,0,2,1:T(2,128)(2,1)} %slice.38) | data formatting | bytes 2097152
  121.4 0.1 copy.63
  121.5 2.7 %gather_fusion = bf16[64,2,4,1024]{3,2,1,0:T(4,128)(2,1)S(1)} fusion(bf16[2,64,4,1024]{3,2,1,0:T(4,128)(2,1)} %copy.74, s32[1024]{0:T(1024)S(1)} %pad_clamp_fusion), kind=kCustom, calls=%fused_computation | custom fusion | bytes 2097408 | tf_op jit(solution)/shard_map/gather | solution.py:122
  124.2 0.6 gather_fusion.1
  124.9 0.9 copy.65
  125.7 0.0 copy-start.5
  125.7 1.7 maximum_bitcast_fusion
  127.4 6.2 %all-to-all-start.1 = ((bf16[2,64,1,4,1025]{4,3,0,2,1:T(4,128)(2,1)}), bf16[2,64,1,4,1025]{4,3,0,2,1:T(4,128)(2,1)S(1)}, u32[]{:S(2)}, u32[]{:S(2)}) async-start(bf16[2,64,1,4,1025]{4,3,0,2,1:T(4,128)(2,1)} %maximum_bitcast_fusion), calls=%async_computation.1 | async-start | bytes 2359296 | tf_op jit(solution)/shard_map/all_to_all | solution.py:27
  133.6 0.0 copy-done.5
  133.6 0.6 fusion.13
  134.2 1.3 compare_and_fusion
  135.5 1.6 multiply_reduce_fusion.1
  137.2 0.0 all-gather.5.cloned.1.call-done
  137.2 1.3 convert_reduce_fusion
  138.4 7.6 %multiply_reduce_fusion = (f32[2]{0:T(128)S(1)}, f32[2,256,1024]{2,1,0:T(8,128)}) fusion(bf16[2,1024,1025]{2,1,0:T(8,128)(2,1)} %all-gather.5.cloned.1.call-done, f32[2,1024]{1,0:T(2,128)S(1)} %convert_reduce_fusion, bf16[2,1024,1024]{2,1,0:T(8,128)(2,1)} %all-gather.3.cloned.1.call-done, bf16[2,256,1024]{2,1,0:T(8,128)(2,1)} %param.15, ...), kind=kOutput, calls=%fused_computation.7 | convolution fusion | flops 2156920832 | bytes 11544584 | tf_op jit(solution)/shard_map/sik,skj->sij/dot_general | solution.py:75
  146.0 7.4 %all-reduce = (f32[2]{0:T(128)S(1)}, f32[2]{0:T(128)S(1)}) all-reduce(f32[2]{0:T(128)S(1)} %get-tuple-element.25, f32[2]{0:T(128)S(1)} %multiply_reduce_fusion.1), channel_id=1, replica_groups=mesh['dp'=64,'mp'=4] {'mp'}, use_global_device_ids=true, to_apply=%region_8.9 | all-reduce | flops 4 | bytes 32 | tf_op jit(solution)/shard_map/psum | solution.py:78
  153.4 2.9 %multiply_convert_fusion.2 = bf16[2,256,1024]{2,1,0:T(8,128)(2,1)} fusion(f32[2,256,1024]{2,1,0:T(8,128)} %get-tuple-element.26, f32[2]{0:T(128)S(1)} %rsqrt_multiply_fusion), kind=kLoop, calls=%fused_computation.6 | loop fusion | flops 1048576 | bytes 3145736 | tf_op jit(solution)/shard_map/convert_element_type | solution.py:80
  156.2 8.7 %all-to-all-done.1 = bf16[2,64,1,4,1025]{4,3,0,2,1:T(4,128)(2,1)S(1)} async-done(((bf16[2,64,1,4,1025]{4,3,0,2,1:T(4,128)(2,1)}), bf16[2,64,1,4,1025]{4,3,0,2,1:T(4,128)(2,1)S(1)}, u32[]{:S(2)}, u32[]{:S(2)}) %all-to-all-start.1) | async-done | bytes 1049632 | tf_op jit(solution)/shard_map/all_to_all | solution.py:27
  164.9 0.9 copy.67
  165.9 1.1 slice_reduce_fusion
  167.0 1.5 fusion.16
  168.5 0.0 copy-start.1
  168.5 0.2 copy.77
  168.7 0.2 copy.78
  168.8 0.6 broadcast_select_fusion.2
  169.5 0.6 copy-done.1
  170.1 2.2 %broadcast_select_fusion = (bf16[2,256,1024]{2,1,0:T(8,128)(2,1)}, bf16[2,256,1024]{2,1,0:T(8,128)(2,1)}) fusion(pred[2]{0:T(512)(128)(4,1)S(1)} %compare_and_fusion, bf16[256,1024]{1,0:T(8,128)(2,1)S(1)} %bitcast.39, bf16[256,1024]{1,0:T(8,128)(2,1)S(1)} %bitcast.40, f32[2,256,1024]{2,1,0:T(8,128)S(1)} %copy-done.1, f32[2,256]{1,0:T(2,128)S(1)} %get-tuple-element.13, ...), kind=kLoop, calls=%fused_computation.23 | loop fusion | flops 3145728 | bytes 7344130 | tf_op jit(solution)/shard_map/jit(_where)/select_n | solution.py:116
  (12 shorter events, 0.1 us)
Async XLA Ops:
  7.2 57.3 %all-gather.3.cloned.1.call-start = ((), (), s32[]{:S(2)}) async-start(), calls=%async_computation.2 | async-start | bytes 5242880 | tf_op jit(solution)/shard_map/all_gather | solution.py:59
  7.9 3.3 %copy-start.8 = (s32[128]{0:T(128)S(1)}, s32[128]{0:T(128)}, u32[]{:S(2)}) copy-start(s32[128]{0:T(128)} %param.19) | copy-start | bytes 1540
  7.9 5.3 %copy-start.3 = (bf16[2,256]{1,0:T(2,128)(2,1)S(1)}, bf16[2,256]{1,0:T(2,128)(2,1)}, u32[]{:S(2)}) copy-start(bf16[2,256]{1,0:T(2,128)(2,1)} %param.12) | copy-start | bytes 3076
  7.9 5.3 %copy-start.4 = (bf16[2,256]{1,0:T(2,128)(2,1)S(1)}, bf16[2,256]{1,0:T(2,128)(2,1)}, u32[]{:S(2)}) copy-start(bf16[2,256]{1,0:T(2,128)(2,1)} %param.14) | copy-start | bytes 3076
  7.9 129.2 %all-gather.5.cloned.1.call-start = ((), (), s32[]{:S(2)}) async-start(), calls=%async_computation.3 | async-start | bytes 5898240 | tf_op jit(solution)/shard_map/all_gather | solution.py:16
  13.9 55.1 %copy-start.2 = (bf16[2,256,1024]{2,1,0:T(8,128)(2,1)S(1)}, bf16[2,256,1024]{2,1,0:T(8,128)(2,1)}, u32[]{:S(2)}) copy-start(bf16[2,256,1024]{2,1,0:T(8,128)(2,1)} %param.10) | copy-start | bytes 3145732
  64.5 4.5 %copy-start.6 = (bf16[2,1024,1024]{2,1,0:T(8,128)(2,1)S(1)}, bf16[2,1024,1024]{2,1,0:T(8,128)(2,1)}, u32[]{:S(2)}) copy-start(bf16[2,1024,1024]{2,1,0:T(8,128)(2,1)} %all-gather.3.cloned.1.call-done) | copy-start | bytes 12582916
  64.5 4.5 %copy-start.7 = (bf16[2,256,1024]{2,1,0:T(8,128)(2,1)S(1)}, bf16[2,256,1024]{2,1,0:T(8,128)(2,1)}, u32[]{:S(2)}) copy-start(bf16[2,256,1024]{2,1,0:T(8,128)(2,1)} %param.11) | copy-start | bytes 3145732
  70.5 1.4 copy-start
  74.4 42.1 %all-to-all-start = ((bf16[2,1,256,1025]{3,0,1,2:T(2,128)(2,1)}), bf16[2,1,256,1025]{3,0,1,2:T(2,128)(2,1)S(1)}, u32[]{:S(2)}, u32[]{:S(2)}) async-start(bf16[2,1,256,1025]{3,0,1,2:T(2,128)(2,1)} %copy.60), calls=%async_computation | async-start | bytes 2359296 | tf_op jit(solution)/shard_map/all_to_all | solution.py:27
  125.7 7.9 %copy-start.5 = (bf16[2,256]{1,0:T(2,128)(2,1)S(1)}, bf16[2,256]{1,0:T(2,128)(2,1)}, u32[]{:S(2)}) copy-start(bf16[2,256]{1,0:T(2,128)(2,1)} %param.16) | copy-start | bytes 3076
  127.4 37.6 %all-to-all-start.1 = ((bf16[2,64,1,4,1025]{4,3,0,2,1:T(4,128)(2,1)}), bf16[2,64,1,4,1025]{4,3,0,2,1:T(4,128)(2,1)S(1)}, u32[]{:S(2)}, u32[]{:S(2)}) async-start(bf16[2,64,1,4,1025]{4,3,0,2,1:T(4,128)(2,1)} %maximum_bitcast_fusion), calls=%async_computation.1 | async-start | bytes 2359296 | tf_op jit(solution)/shard_map/all_to_all | solution.py:27
  168.5 1.6 copy-start.1
Sparse Core Ops, SparseCore 0:
  9.8 54.5 all-gather.2
  66.3 55.5 all-gather.4
where the time goes:
time: 180 us; the launch traced here: 179 us
  waiting for transfers between devices  91.2 us (51%)
  local copies, waits for them, and re-layouts  17.7 us (10%)
  starting transfers between devices  17 us (9%)
  between operations  16.3 us (9%)
  other arithmetic  16 us (9%)
  matrix products  13.6 us (8%)
  blocking collectives  7.38 us (4%)
    all_gather x1, waiting for transfers between devices, refresh(): gathered = lax.all_gather(gradient, 'mp', axis=1, tiled=True)  50.6 us
    all_to_all x2, waiting for transfers between devices, in_one_piece(): lax.all_to_all(both, axis, split_axis=split_dim, concat_axis=concat_dim,...  39.9 us
    all_to_all x2, starting transfers between devices, in_one_piece(): lax.all_to_all(both, axis, split_axis=split_dim, concat_axis=concat_dim,...  16.9 us
    dot_general x1, matrix products, refresh(): jnp.einsum('sik,skj->sij', lifted, root_piece, preferred_element_type=jnp...  7.56 us
    psum x1, blocking collectives, refresh(): grad_total, dir_total = lax.psum((grad_square, dir_square), 'mp')  7.38 us
    dot_general x1, matrix products, refresh(): jnp.einsum('sji,sjk->sik', columns, gathered, preferred_element_type=jnp....  4.49 us
    unnamed x21, local copies, waits for them, and re-layouts  4.16 us
  transfers between devices with their start and end apart: 4, of which 3 were waited for; matrix products, arithmetic and copies ran while one was open for 22% of the time, Pallas kernels for 0%

commit v1 on v0

--- a/solution.py
+++ b/solution.py
@@ -6,6 +6,14 @@
 
 DECAY = 0.95
 EPSILON = 1e-06
+
+
+def gather_by_exchange(array, axis, dim):
+    length = lax.axis_size(axis)
+    repeats = [length if d == dim else 1 for d in range(array.ndim)]
+    return lax.all_to_all(
+        jnp.tile(array, repeats), axis, split_axis=dim, concat_axis=dim, tiled=True
+    )
 
 
 def side_by_side(arrays, axis, dim, along):
@@ -56,7 +64,7 @@
     right_root_codes,
     right_root_scales,
 ):
-    gathered = lax.all_gather(gradient, "mp", axis=1, tiled=True)
+    gathered = gather_by_exchange(gradient, "mp", 1)
     height = gradient.shape[1]
     offset = lax.axis_index("mp") * height
     left_new = DECAY * dequantize(left_codes, left_scales) + jnp.einsum(

time: 180 us -> 216 us (1.20)
  starting transfers between devices: 17 us -> 32.2 us
  waiting for transfers between devices: 91.2 us -> 105 us
  local copies, waits for them, and re-layouts: 17.7 us -> 23.2 us
  matrix products: 13.6 us -> 16.6 us
    all_to_all x0 -> x1, waiting for transfers between devices: none -> 65.6 us  [gather_by_exchange(): lax.all_to_all(jnp.tile(array, repeats), axis, split_axis=dim, concat_axi...]
    all_gather x1 -> x0, waiting for transfers between devices: 50.6 us -> none  [refresh(): gathered = lax.all_gather(gradient, 'mp', axis=1, tiled=True)]
    all_to_all x2, starting transfers between devices: 16.9 us -> 27 us  [in_one_piece(): lax.all_to_all(both, axis, split_axis=split_dim, concat_axis=concat_dim,...]
    all_to_all x0 -> x1, starting transfers between devices: none -> 5.14 us  [gather_by_exchange(): lax.all_to_all(jnp.tile(array, repeats), axis, split_axis=dim, concat_axi...]
    another operation x0 -> x1, local copies, waits for them, and re-layouts: none -> 4.15 us  [gather_by_exchange(): jnp.tile(array, repeats)]
    dot_general x1, matrix products: 1.55 us -> 4.25 us  [refresh(): jnp.einsum('sik,sjk->sij', gradient, gathered, preferred_element_type=jnp...]
    unnamed x21 -> x26, local copies, waits for them, and re-layouts: 4.16 us -> 5.25 us
  transfers between devices with their start and end apart: 4 -> 4, of which waited for: 3 -> 3; matrix products, arithmetic and copies ran while one was open for 22% -> 19% of each run, Pallas kernels for 0% -> 0%
where the time goes in v1:
time: 216 us; the launch traced here: 215 us
  waiting for transfers between devices  105 us (49%)
  starting transfers between devices  32.2 us (15%)
  local copies, waits for them, and re-layouts  23.2 us (11%)
  matrix products  16.6 us (8%)
  between operations  16.3 us (8%)
  other arithmetic  14.8 us (7%)
  blocking collectives  6.98 us (3%)
    all_to_all x1, waiting for transfers between devices, gather_by_exchange(): lax.all_to_all(jnp.tile(array, repeats), axis, split_axis=dim, concat_axi...  65.6 us
    all_to_all x2, waiting for transfers between devices, in_one_piece(): lax.all_to_all(both, axis, split_axis=split_dim, concat_axis=concat_dim,...  39.9 us
    all_to_all x2, starting transfers between devices, in_one_piece(): lax.all_to_all(both, axis, split_axis=split_dim, concat_axis=concat_dim,...  27 us
    dot_general x1, matrix products, refresh(): jnp.einsum('sik,skj->sij', lifted, root_piece, preferred_element_type=jnp...  8 us
    psum x1, blocking collectives, refresh(): grad_total, dir_total = lax.psum((grad_square, dir_square), 'mp')  6.98 us
    unnamed x26, local copies, waits for them, and re-layouts  5.25 us
    all_to_all x1, starting transfers between devices, gather_by_exchange(): lax.all_to_all(jnp.tile(array, repeats), axis, split_axis=dim, concat_axi...  5.14 us
  transfers between devices with their start and end apart: 4, of which 3 were waited for; matrix products, arithmetic and copies ran while one was open for 19% of the time, Pallas kernels for 0%

profile of v1, /device:TPU:1, one launch (start us, length us, event | category | flops | bytes accessed | tf_op | source)
XLA Modules:
  0.0 215.4 jit_solution(11712908547199569430)
XLA Ops:
  7.2 2.3 %copy.66 = bf16[2,256,1024]{2,0,1:T(2,128)(2,1)S(1)} copy(bf16[2,256,1024]{2,1,0:T(8,128)(2,1)} %param.10) | data formatting | bytes 2097152 | tf_op args[0]
  9.5 4.2 %tile.4 = bf16[2,4,256,1024]{3,0,2,1:T(2,128)(2,1)} broadcast(bf16[2,256,1024]{2,0,1:T(2,128)(2,1)S(1)} %copy.66), dimensions={0,2,3} | broadcast | bytes 5242880 | tf_op jit(solution)/shard_map/tile | solution.py:15
  13.6 0.0 copy-start.4
  13.6 0.0 copy-start.3
  13.6 5.1 %all-to-all-start = ((bf16[2,1024,1024]{2,0,1:T(2,128)(2,1)}), bf16[2,1024,1024]{2,0,1:T(2,128)(2,1)}, u32[]{:S(2)}, u32[]{:S(2)}) async-start(bf16[2,1024,1024]{2,0,1:T(2,128)(2,1)} %bitcast.32), calls=%async_computation | async-start | bytes 8388608 | tf_op jit(solution)/shard_map/all_to_all | solution.py:14
  18.8 0.0 copy-start.10
  18.8 0.0 copy-start.5
  18.8 0.0 all-gather.2.cloned.1.call-start
  18.8 0.0 copy-done.4
  18.8 0.2 copy.80
  19.0 0.0 copy-done.3
  19.0 1.1 pad_maximum_fusion.1
  20.2 0.0 all-gather.2.cloned.1.call-update
  20.2 0.0 copy-done.10
  20.2 0.6 fusion.24
  22.2 0.0 copy-done.5
  22.2 0.0 copy-done.6
  22.9 65.6 %all-to-all-done = bf16[2,1024,1024]{2,0,1:T(2,128)(2,1)} async-done(((bf16[2,1024,1024]{2,0,1:T(2,128)(2,1)}), bf16[2,1024,1024]{2,0,1:T(2,128)(2,1)}, u32[]{:S(2)}, u32[]{:S(2)}) %all-to-all-start) | async-done | bytes 4194336 | tf_op jit(solution)/shard_map/all_to_all | solution.py:14
  88.4 2.0 constant_dynamic-slice_fusion.2
  90.4 0.0 copy-done.8
  90.4 0.0 copy-start.2
  90.4 0.0 copy-start.9
  90.4 4.3 %abs_reduce_fusion = (f32[2,256]{1,0:T(2,128)S(1)}, f32[2,256,1024]{2,1,0:T(8,128)S(1)}) fusion(bf16[2,1024,1024]{2,0,1:T(2,128)(2,1)} %all-to-all-done, bf16[2,1024,256]{2,0,1:T(2,128)(2,1)S(1)} %constant_dynamic-slice_fusion.2, f32[2,256]{1,0:T(2,128)S(1)} %convert_element_type.78, bf16[2,256,1024]{2,1,0:T(8,128)(2,1)S(1)} %copy-done.8), kind=kOutput, calls=%fused_computation.17 | convolution fusion | flops 1076887040 | bytes 8392704 | tf_op jit(solution)/shard_map/sji,sjk->sik/dot_general | solution.py:74
  94.8 0.0 copy-done.2
  94.8 0.0 copy-done.9
  94.8 4.3 %abs_reduce_fusion.1 = (f32[2,256]{1,0:T(2,128)S(1)}, f32[2,256,1024]{2,1,0:T(8,128)S(1)}) fusion(bf16[2,256,1024]{2,1,0:T(8,128)(2,1)S(1)} %copy-done.2, bf16[2,1024,1024]{2,0,1:T(2,128)(2,1)} %all-to-all-done, f32[2,256]{1,0:T(2,128)S(1)} %convert_element_type.73, bf16[2,256,1024]{2,1,0:T(8,128)(2,1)S(1)} %copy-done.9), kind=kOutput, calls=%fused_computation.20 | convolution fusion | flops 1076887040 | bytes 8392704 | tf_op jit(solution)/shard_map/sik,sjk->sij/dot_general | solution.py:70
  99.1 0.1 reshape.127
  99.2 0.3 divide_convert_fusion
  99.5 0.3 divide_convert_fusion.1
  99.8 0.6 copy-done
  100.4 0.1 dynamic-slice_bitcast_fusion
  100.5 0.1 pad_maximum_fusion
  100.6 2.2 %copy.71 = bf16[2,1,256,1025]{3,0,1,2:T(2,128)(2,1)} copy(bf16[2,1,256,1025]{3,2,1,0:T(8,128)(2,1)S(1)} %pad_maximum_fusion) | data formatting | bytes 2099200 | tf_op jit(solution)/shard_map/concatenate | solution.py:33
  102.8 20.8 %all-to-all-start.1 = ((bf16[2,1,256,1025]{3,0,1,2:T(2,128)(2,1)}), bf16[2,1,256,1025]{3,0,1,2:T(2,128)(2,1)S(1)}, u32[]{:S(2)}, u32[]{:S(2)}) async-start(bf16[2,1,256,1025]{3,0,1,2:T(2,128)(2,1)} %copy.71), calls=%async_computation.1 | async-start | bytes 2359296 | tf_op jit(solution)/shard_map/all_to_all | solution.py:35
  123.6 0.1 select_reduce_fusion
  123.8 31.2 %all-to-all-done.1 = bf16[2,1,256,1025]{3,0,1,2:T(2,128)(2,1)S(1)} async-done(((bf16[2,1,256,1025]{3,0,1,2:T(2,128)(2,1)}), bf16[2,1,256,1025]{3,0,1,2:T(2,128)(2,1)S(1)}, u32[]{:S(2)}, u32[]{:S(2)}) %all-to-all-start.1) | async-done | bytes 1049632 | tf_op jit(solution)/shard_map/all_to_all | solution.py:35
  155.0 1.1 slice.38
  156.1 0.1 slice.39
  156.2 1.4 copy.86
  157.6 0.1 copy.73
  157.7 0.1 copy.74
  157.9 2.7 %gather_fusion = bf16[64,2,4,1024]{3,2,1,0:T(4,128)(2,1)S(1)} fusion(bf16[2,64,4,1024]{3,2,1,0:T(4,128)(2,1)} %copy.86, s32[1024]{0:T(1024)S(1)} %pad_clamp_fusion), kind=kCustom, calls=%fused_computation | custom fusion | bytes 2097408 | tf_op jit(solution)/shard_map/gather | solution.py:130
  160.6 0.6 gather_fusion.1
  161.2 0.9 copy.76
  162.1 1.6 maximum_bitcast_fusion
  163.7 6.2 %all-to-all-start.2 = ((bf16[2,64,1,4,1025]{4,3,0,2,1:T(4,128)(2,1)}), bf16[2,64,1,4,1025]{4,3,0,2,1:T(4,128)(2,1)S(1)}, u32[]{:S(2)}, u32[]{:S(2)}) async-start(bf16[2,64,1,4,1025]{4,3,0,2,1:T(4,128)(2,1)} %maximum_bitcast_fusion), calls=%async_computation.2 | async-start | bytes 2359296 | tf_op jit(solution)/shard_map/all_to_all | solution.py:35
  169.9 0.0 copy-done.7
  169.9 0.6 fusion.27
  170.6 1.3 compare_and_fusion
  171.9 1.6 multiply_reduce_fusion.1
  173.5 1.3 convert_reduce_fusion
  174.7 8.0 %multiply_reduce_fusion = (f32[2]{0:T(128)S(1)}, f32[2,256,1024]{2,1,0:T(8,128)}) fusion(bf16[2,1024,1025]{2,1,0:T(8,128)(2,1)} %all-gather.2.cloned.1.call-done, f32[2,1024]{1,0:T(2,128)S(1)} %convert_reduce_fusion, bf16[2,1024,1024]{2,0,1:T(2,128)(2,1)} %all-to-all-done, bf16[2,256,1024]{2,1,0:T(8,128)(2,1)} %param.15, f32[2,256]{1,0:T(2,128)S(1)} %convert_element_type.83), kind=kOutput, calls=%fused_computation.13 | convolution fusion | flops 2156920832 | bytes 11544584 | tf_op jit(solution)/shard_map/sik,skj->sij/dot_general | solution.py:83
  182.7 7.0 %all-reduce = (f32[2]{0:T(128)S(1)}, f32[2]{0:T(128)S(1)}) all-reduce(f32[2]{0:T(128)S(1)} %get-tuple-element.25, f32[2]{0:T(128)S(1)} %multiply_reduce_fusion.1), channel_id=1, replica_groups=mesh['dp'=64,'mp'=4] {'mp'}, use_global_device_ids=true, to_apply=%region_8.9 | all-reduce | flops 4 | bytes 32 | tf_op jit(solution)/shard_map/psum | solution.py:86
  189.7 2.9 %multiply_convert_fusion.2 = bf16[2,256,1024]{2,1,0:T(8,128)(2,1)} fusion(f32[2,256,1024]{2,1,0:T(8,128)} %get-tuple-element.26, f32[2]{0:T(128)S(1)} %rsqrt_multiply_fusion), kind=kLoop, calls=%fused_computation.12 | loop fusion | flops 1048576 | bytes 3145736 | tf_op jit(solution)/shard_map/convert_element_type | solution.py:88
  192.6 8.7 %all-to-all-done.2 = bf16[2,64,1,4,1025]{4,3,0,2,1:T(4,128)(2,1)S(1)} async-done(((bf16[2,64,1,4,1025]{4,3,0,2,1:T(4,128)(2,1)}), bf16[2,64,1,4,1025]{4,3,0,2,1:T(4,128)(2,1)S(1)}, u32[]{:S(2)}, u32[]{:S(2)}) %all-to-all-start.2) | async-done | bytes 1049632 | tf_op jit(solution)/shard_map/all_to_all | solution.py:35
  201.3 0.9 copy.78
  202.2 1.1 slice_reduce_fusion
  203.3 1.5 fusion.30
  204.8 0.0 copy-start.1
  204.8 0.2 copy.113
  205.0 0.2 copy.114
  205.2 0.6 broadcast_select_fusion.2
  205.8 0.6 copy-done.1
  206.4 2.2 %broadcast_select_fusion = (bf16[2,256,1024]{2,1,0:T(8,128)(2,1)}, bf16[2,256,1024]{2,1,0:T(8,128)(2,1)}) fusion(pred[2]{0:T(512)(128)(4,1)S(1)} %compare_and_fusion, bf16[256,1024]{1,0:T(8,128)(2,1)S(1)} %bitcast.38, bf16[256,1024]{1,0:T(8,128)(2,1)S(1)} %bitcast.39, f32[2,256,1024]{2,1,0:T(8,128)S(1)} %copy-done.1, f32[2,256]{1,0:T(2,128)S(1)} %get-tuple-element.13, ...), kind=kLoop, calls=%fused_computation.29 | loop fusion | flops 3145728 | bytes 7344130 | tf_op jit(solution)/shard_map/jit(_where)/select_n | solution.py:124
  (17 shorter events, 0.1 us)
Async XLA Ops:
  13.6 5.2 %copy-start.4 = (bf16[2,256]{1,0:T(2,128)(2,1)S(1)}, bf16[2,256]{1,0:T(2,128)(2,1)}, u32[]{:S(2)}) copy-start(bf16[2,256]{1,0:T(2,128)(2,1)} %param.18) | copy-start | bytes 3076
  13.6 5.4 %copy-start.3 = (bf16[2,256,1024]{2,1,0:T(8,128)(2,1)S(1)}, bf16[2,256,1024]{2,1,0:T(8,128)(2,1)}, u32[]{:S(2)}) copy-start(bf16[2,256,1024]{2,1,0:T(8,128)(2,1)} %param.17) | copy-start | bytes 3145732
  13.6 74.8 %all-to-all-start = ((bf16[2,1024,1024]{2,0,1:T(2,128)(2,1)}), bf16[2,1024,1024]{2,0,1:T(2,128)(2,1)}, u32[]{:S(2)}, u32[]{:S(2)}) async-start(bf16[2,1024,1024]{2,0,1:T(2,128)(2,1)} %bitcast.32), calls=%async_computation | async-start | bytes 8388608 | tf_op jit(solution)/shard_map/all_to_all | solution.py:14
  18.8 1.4 copy-start.10
  18.8 3.4 %copy-start.5 = (bf16[2,256]{1,0:T(2,128)(2,1)S(1)}, bf16[2,256]{1,0:T(2,128)(2,1)}, u32[]{:S(2)}) copy-start(bf16[2,256]{1,0:T(2,128)(2,1)} %param.14) | copy-start | bytes 3076
  18.8 3.4 %copy-start.6 = (bf16[2,256]{1,0:T(2,128)(2,1)S(1)}, bf16[2,256]{1,0:T(2,128)(2,1)}, u32[]{:S(2)}) copy-start(bf16[2,256]{1,0:T(2,128)(2,1)} %param.12) | copy-start | bytes 3076
  18.8 154.7 %all-gather.2.cloned.1.call-start = ((), (), s32[]{:S(2)}) async-start(), calls=%async_computation.3 | async-start | bytes 5898240 | tf_op jit(solution)/shard_map/all_gather | solution.py:24
  20.2 70.2 %copy-start.8 = (bf16[2,256,1024]{2,1,0:T(8,128)(2,1)S(1)}, bf16[2,256,1024]{2,1,0:T(8,128)(2,1)}, u32[]{:S(2)}) copy-start(bf16[2,256,1024]{2,1,0:T(8,128)(2,1)} %param.13) | copy-start | bytes 3145732
  90.4 4.4 %copy-start.2 = (bf16[2,256,1024]{2,1,0:T(8,128)(2,1)S(1)}, bf16[2,256,1024]{2,1,0:T(8,128)(2,1)}, u32[]{:S(2)}) copy-start(bf16[2,256,1024]{2,1,0:T(8,128)(2,1)} %param.10) | copy-start | bytes 3145732
  90.4 4.4 %copy-start.9 = (bf16[2,256,1024]{2,1,0:T(8,128)(2,1)S(1)}, bf16[2,256,1024]{2,1,0:T(8,128)(2,1)}, u32[]{:S(2)}) copy-start(bf16[2,256,1024]{2,1,0:T(8,128)(2,1)} %param.11) | copy-start | bytes 3145732
  99.0 1.4 copy-start
  102.8 52.2 %all-to-all-start.1 = ((bf16[2,1,256,1025]{3,0,1,2:T(2,128)(2,1)}), bf16[2,1,256,1025]{3,0,1,2:T(2,128)(2,1)S(1)}, u32[]{:S(2)}, u32[]{:S(2)}) async-start(bf16[2,1,256,1025]{3,0,1,2:T(2,128)(2,1)} %copy.71), calls=%async_computation.1 | async-start | bytes 2359296 | tf_op jit(solution)/shard_map/all_to_all | solution.py:35
  162.1 7.8 %copy-start.7 = (bf16[2,256]{1,0:T(2,128)(2,1)S(1)}, bf16[2,256]{1,0:T(2,128)(2,1)}, u32[]{:S(2)}) copy-start(bf16[2,256]{1,0:T(2,128)(2,1)} %param.16) | copy-start | bytes 3076
  163.7 37.6 %all-to-all-start.2 = ((bf16[2,64,1,4,1025]{4,3,0,2,1:T(4,128)(2,1)}), bf16[2,64,1,4,1025]{4,3,0,2,1:T(4,128)(2,1)S(1)}, u32[]{:S(2)}, u32[]{:S(2)}) async-start(bf16[2,64,1,4,1025]{4,3,0,2,1:T(4,128)(2,1)} %maximum_bitcast_fusion), calls=%async_computation.2 | async-start | bytes 2359296 | tf_op jit(solution)/shard_map/all_to_all | solution.py:35
  204.8 1.6 copy-start.1
Sparse Core Ops, SparseCore 0:
  21.4 85.3 all-gather.1
